TPU v7x, 32 devices: a whole 2x2x4 slice. The times are simulated.
32 devices in a mesh: tier: 4 (over x, core), tile: 8 (over z, y).
Axes of the slice: x: 2, y: 2, z: 4, core: 2. Of those that a mesh axis runs over, the one named last changes fastest.
Arguments:
- starting_warmth_rise: float32 [32, 96, 1024], P('tile', 'tier'), may hold values from -3 to 8
- substance_per_cell: int32 [32, 96, 1024], P('tile', 'tier'), may hold values from 0 to 7
- material_transport_rates: float32 [2, 8], replicated, may hold values from 0.2 to 2
- patch_region_label: int32 [8, 8], P('tile'), may hold values from 0 to 15, as said below
- static_power_per_area: float32 [4, 16], replicated, may hold values from 0.5 to 4
- warming_power_factor: float32 [4, 16], replicated, may hold values from 0.2 to 0.8
- stacking_solve_operator: float32 [96, 96], replicated, may hold values from 0 to 1
Outputs:
- final_temperature: float32 [32, 96, 1024], P('tile', 'tier')
- block_power: float32 [4, 16], P('tier')
Inputs may be any that keep to these rules, and one draw needn't show every extreme that they name: `patch_region_label`: every block number names at least one tile.
All inputs are finite; a program needn't handle non-finite values.
Results may differ from a plain program's by a relative error of at most 0.0001.
Values sent between devices are 32-bit elements; how exact they have to be, the bound alone decides.
A program may use at most 64 MiB of HBM per device.

v0:
```python
import jax
import jax.numpy as jnp
from jax import lax
from jax.sharding import PartitionSpec as P

TILE_COLS = 128
STEPS = 2
LATERAL_RATE = 0.12
SOURCE_GAIN = 0.02


def extended(block, sides, width):
    for axis, dim in sides:
        count = lax.axis_size(axis)
        forward = [(i, i + 1) for i in range(count - 1)]
        backward = [(target, source) for source, target in forward]
        low = lax.ppermute(
            lax.slice_in_dim(block, block.shape[dim] - width, None, axis=dim), axis, forward
        )
        high = lax.ppermute(lax.slice_in_dim(block, 0, width, axis=dim), axis, backward)
        block = jnp.concatenate([low, block, high], axis=dim)
    return block


def pair_mean(cond_a, cond_b):
    return 2.0 * cond_a * cond_b / (cond_a + cond_b)


def lateral(padded, conduct):
    centre = padded[1:-1, :, 1:-1]
    sideways_coupling_rate = conduct[0, 1:-1, :, 1:-1]
    stacking_coupling_rate = conduct[1, 1:-1, :, 1:-1]
    flow_sum = pair_mean(sideways_coupling_rate, conduct[0, 2:, :, 1:-1]) * (
        padded[2:, :, 1:-1] - centre
    )
    flow_sum = flow_sum + pair_mean(sideways_coupling_rate, conduct[0, :-2, :, 1:-1]) * (
        padded[:-2, :, 1:-1] - centre
    )
    flow_sum = flow_sum + pair_mean(stacking_coupling_rate, conduct[1, 1:-1, :, 2:]) * (
        padded[1:-1, :, 2:] - centre
    )
    flow_sum = flow_sum + pair_mean(stacking_coupling_rate, conduct[1, 1:-1, :, :-2]) * (
        padded[1:-1, :, :-2] - centre
    )
    return centre + LATERAL_RATE * flow_sum


def exact_dot(left_op, right_op):
    return jnp.dot(
        left_op, right_op, precision=lax.Precision.HIGHEST, preferred_element_type=jnp.float32
    )


def lookup_codes(codes, material_transport_rates):
    sideways_coupling_rate = jnp.zeros(codes.shape, jnp.float32)
    stacking_coupling_rate = jnp.zeros(codes.shape, jnp.float32)
    for material in range(material_transport_rates.shape[1]):
        is_material = codes == material + 1
        sideways_coupling_rate = jnp.where(
            is_material, material_transport_rates[0, material], sideways_coupling_rate
        )
        stacking_coupling_rate = jnp.where(
            is_material, material_transport_rates[1, material], stacking_coupling_rate
        )
    return jnp.stack([sideways_coupling_rate, stacking_coupling_rate])


def tile_partials(active, tile_hot):
    mesh_height_cells, groups, col_count = active.shape
    quarter = col_count // TILE_COLS
    tile_sums = active.reshape(mesh_height_cells, groups, quarter, TILE_COLS).sum(axis=(0, 3))
    partial_value = exact_dot(tile_sums, tile_hot)
    counts = float(mesh_height_cells * TILE_COLS) * jnp.sum(tile_hot, axis=0)
    return (partial_value, counts)


def spread_power(block_power, tile_hot, mesh_height_cells):
    tile_power = exact_dot(block_power, tile_hot.T)
    groups, quarter = tile_power.shape
    cells = jnp.broadcast_to(
        tile_power[None, :, :, None], (mesh_height_cells, groups, quarter, TILE_COLS)
    )
    return cells.reshape(mesh_height_cells, groups, quarter * TILE_COLS)


def leak_tiers(active, tile_hot, static_power_per_area, warming_power_factor, tier_id):
    partial_value, counts = tile_partials(active, tile_hot)
    block_sum, block_count = lax.psum((partial_value[0], counts), "tile")
    base_row = lax.dynamic_slice_in_dim(static_power_per_area, tier_id, 1, 0)
    slope_row = lax.dynamic_slice_in_dim(warming_power_factor, tier_id, 1, 0)
    return base_row * jnp.exp(slope_row * block_sum[None, :] / block_count[None, :])


def shards(
    starting_warmth_rise,
    substance_per_cell,
    material_transport_rates,
    patch_region_label,
    static_power_per_area,
    warming_power_factor,
    stacking_solve_operator,
):
    mesh_height_cells, stacked_layer_number, lateral_width_cells = starting_warmth_rise.shape
    tier_id = lax.axis_index("tier")
    block_total = static_power_per_area.shape[1]
    codes = substance_per_cell + 1
    block_range = jnp.arange(block_total, dtype=jnp.int32)
    cond_pad = extended(lookup_codes(codes, material_transport_rates), (("tile", 1),), 1)
    cond_pad = jnp.pad(cond_pad, ((0, 0), (0, 0), (0, 0), (1, 1)))
    tile_hot = (patch_region_label[0][:, None] == block_range[None, :]).astype(jnp.float32)
    present_warming_state = starting_warmth_rise
    power_row = jnp.zeros((1, block_total), jnp.float32)
    for step_index in range(STEPS):
        padded = extended(present_warming_state, (("tile", 0),), 1)
        padded = jnp.pad(padded, ((0, 0), (0, 0), (1, 1)))
        power_row = leak_tiers(
            present_warming_state[:, ::stacked_layer_number, :],
            tile_hot,
            static_power_per_area,
            warming_power_factor,
            tier_id,
        )
        moved_field = lateral(padded, cond_pad)
        moved_field = moved_field.at[:, ::stacked_layer_number, :].add(
            SOURCE_GAIN * spread_power(power_row, tile_hot, mesh_height_cells)
        )
        applied = jnp.einsum(
            "lm,rmc->rlc",
            stacking_solve_operator,
            lax.all_to_all(moved_field, "tier", split_axis=2, concat_axis=1, tiled=True),
            precision=lax.Precision.HIGHEST,
        )
        present_warming_state = lax.all_to_all(
            applied, "tier", split_axis=1, concat_axis=2, tiled=True
        )
    return (present_warming_state, power_row)


def solution(mesh):
    in_specs = (
        P("tile", "tier", None),
        P("tile", "tier", None),
        P(),
        P("tile", None),
        P(),
        P(),
        P(),
    )
    out_specs = (P("tile", "tier", None), P("tier", None))
    return jax.shard_map(shards, mesh=mesh, in_specs=in_specs, out_specs=out_specs, check_vma=False)
```

profile of v0, /device:TPU:8, one launch (start us, length us, event | category | flops | bytes accessed | tf_op | source)
XLA Modules:
  0.0 144.2 jit_solution(3918848064363869905)
XLA Ops:
  0.6 0.0 copy-start
  0.6 1.0 fusion.41
  1.6 3.4 %collective-permute-start.3 = (f32[1,24,1024]{2,1,0:T(8,128)S(1)}, f32[1,24,1024]{2,1,0:T(8,128)S(1)}, u32[]{:S(2)}, u32[]{:S(2)}) collective-permute-start(f32[1,24,1024]{2,1,0:T(8,128)S(1)} %get-tuple-element.44), channel_id=1, source_target_pairs={{0,1},{1,2},{2,3},{3,4},{4,5},{5,6},{6,7},{8,9},{9,10},{10,11},{11... | collective-permute-start | bytes 294920 | tf_op jit(solution)/shard_map/ppermute | solution.py:17
  5.0 3.3 %collective-permute-start.1 = (f32[1,24,1024]{2,1,0:T(8,128)S(1)}, f32[1,24,1024]{2,1,0:T(8,128)S(1)}, u32[]{:S(2)}, u32[]{:S(2)}) collective-permute-start(f32[1,24,1024]{2,1,0:T(8,128)S(1)} %get-tuple-element.45), channel_id=1, source_target_pairs={{1,0},{2,1},{3,2},{4,3},{5,4},{6,5},{7,6},{9,8},{10,9},{11,10},{12... | collective-permute-start | bytes 294920 | tf_op jit(solution)/shard_map/ppermute | solution.py:20
  8.4 2.0 %fusion.42 = (f32[1,1]{1,0:T(1,128)}, f32[1,1]{1,0:T(1,128)}, f32[1,1]{1,0:T(1,128)}, f32[1,1]{1,0:T(1,128)}, f32[1,1]{1,0:T(1,128)}, /*index=5*/f32[1,1]{1,0:T(...) fusion(f32[2,8]{1,0:T(2,128)} %param.13), kind=kLoop, calls=%fused_computation.105 | loop fusion | bytes 128 | tf_op jit(solution)/shard_map/slice | solution.py:60
  10.3 6.6 %select_select_fusion = (f32[4,24,1024]{2,1,0:T(8,128)S(1)}, pred[4,24,1024]{2,1,0:T(8,128)(4,1)S(1)}, pred[4,24,1024]{2,1,0:T(8,128)(4,1)S(1)}, pred[4,24,1024]...) fusion(f32[]{:T(128)} %bitcast.16, f32[]{:T(128)} %bitcast.15, ...), kind=kLoop, calls=%fused_computation.62 | loop fusion | flops 1671168 | bytes 1572896 | tf_op jit(solution)/shard_map/jit(_where)/select_n | solution.py:62
  16.9 0.0 copy-start.3
  16.9 0.0 copy-start.7
  16.9 0.0 copy-start.5
  16.9 0.0 copy-start.6
  17.0 5.4 %select_select_fusion.1 = f32[4,24,1024]{2,1,0:T(8,128)S(1)} fusion(pred[4,24,1024]{2,1,0:T(8,128)(4,1)S(1)} %get-tuple-element.39, pred[4,24,1024]{2,1,0:T(8,128)(4,1)S(1)} %get-tuple-element.38, pred[4,24,1024]{2,1,0:T(8,128)(4,1)S(1)} %get-tuple-element.37, pred[4,24,1024]{2,1,0:T(8,128)(4,1)S(1)} %get-tuple-element.36, ...), kind=kLoop, calls=%fused_computation.63 | loop fusion | flops 786432 | bytes 1179680 | tf_op jit(solution)/shard_map/jit(_where)/select_n | solution.py:59
  22.4 2.5 %collective-permute-start.2 = (f32[2,1,24,1024]{3,2,1,0:T(8,128)S(1)}, f32[2,1,24,1024]{3,2,1,0:T(8,128)S(1)}, u32[]{:S(2)}, u32[]{:S(2)}) collective-permute-start(f32[2,1,24,1024]{3,2,1,0:T(8,128)S(1)} %get-tuple-element.40), channel_id=1, source_target_pairs={{0,1},{1,2},{2,3},{3,4},{4,5},{5,6},{6,7},{8,9},{9,10},{10,11},{11... | collective-permute-start | bytes 589832 | tf_op jit(solution)/shard_map/ppermute | solution.py:17
  24.9 4.2 %collective-permute-start = (f32[2,1,24,1024]{3,2,1,0:T(8,128)S(1)}, f32[2,1,24,1024]{3,2,1,0:T(8,128)S(1)}, u32[]{:S(2)}, u32[]{:S(2)}) collective-permute-start(f32[2,1,24,1024]{3,2,1,0:T(8,128)S(1)} %get-tuple-element.41), channel_id=1, source_target_pairs={{1,0},{2,1},{3,2},{4,3},{5,4},{6,5},{7,6},{9,8},{10,9},{11,10},{12... | collective-permute-start | bytes 589832 | tf_op jit(solution)/shard_map/ppermute | solution.py:20
  29.2 0.1 convert_reduce_fusion
  29.3 0.1 bitcast_reduce_fusion.1
  29.4 0.2 fusion.31
  29.6 17.1 %all-reduce.3 = (f32[1,16]{1,0:T(1,128)S(1)}, f32[1,16]{1,0:T(1,128)S(1)}) all-reduce(f32[1,16]{1,0:T(1,128)S(1)} %multiply_bitcast_fusion.2, f32[1,16]{1,0:T(1,128)S(1)} %fusion.31), channel_id=1, replica_groups=mesh['tier'=4,'tile'=8] {'tile'}, use_global_device_ids=true, to_apply=%region_4.5 | all-reduce | flops 32 | bytes 256 | tf_op jit(solution)/shard_map/psum | solution.py:88
  46.7 0.2 fusion.1
  46.8 0.1 broadcast_bitcast_fusion.1
  46.9 0.0 collective-permute-done.3
  46.9 0.0 collective-permute-done.1
  46.9 0.3 select_maximum_fusion.5
  47.2 0.0 collective-permute-done.2
  47.2 0.4 select_maximum_fusion
  47.6 1.2 fusion.18
  48.9 0.1 scatter-add.6
  49.0 0.9 copy.88
  49.9 2.9 %reshape.124 = f32[4,1,24576]{2,1,0:T(1,128)S(1)} reshape(f32[1024,4,24]{2,1,0:T(4,128)S(1)} %bitcast.115) | data formatting | bytes 786432
  52.8 10.0 %all_to_all.72 = f32[4,1,24576]{2,1,0:T(1,128)S(1)} all-to-all(f32[4,1,24576]{2,1,0:T(1,128)S(1)} %reshape.124), channel_id=1, replica_groups=mesh['tier'=4,'tile'=8] {'tier'}, dimensions={0} | all-to-all | bytes 786432 | tf_op jit(solution)/shard_map/all_to_all | solution.py:130
  62.8 0.5 broadcast.157
  63.3 1.7 %reduce.10 = f32[4,24576]{1,0:T(4,128)S(1)} reduce(f32[4,1,24576]{2,1,0:T(1,128)S(1)} %all_to_all.72, f32[]{:T(128)} %broadcast.157), dimensions={1}, to_apply=%all_to_all.52.reduce_sub_computation | reduce | bytes 786436 | tf_op jit(solution)/shard_map/all_to_all | solution.py:130
  65.0 2.8 %reshape.125 = f32[1024,4,24]{2,1,0:T(4,128)S(1)} reshape(f32[4,24576]{1,0:T(4,128)S(1)} %reduce.10) | data formatting | bytes 786432
  67.8 0.8 copy.89
  68.6 0.5 convolution_bitcast_fusion.1
  69.1 0.3 copy.90
  69.4 9.8 %all_to_all.73 = f32[4,96,256]{2,0,1:T(4,128)S(1)} all-to-all(f32[4,96,256]{2,0,1:T(4,128)S(1)} %copy.90), channel_id=1, replica_groups=mesh['tier'=4,'tile'=8] {'tier'}, dimensions={1} | all-to-all | bytes 786432 | tf_op jit(solution)/shard_map/all_to_all | solution.py:133
  79.2 0.3 copy.97
  79.5 0.2 all_to_all.59
  79.7 0.1 bitcast_reduce_fusion
  79.8 0.2 fusion.30
  80.0 0.1 slice.222
  80.1 17.1 %psum.26 = f32[1,16]{1,0:T(1,128)S(1)} all-reduce(f32[1,16]{1,0:T(1,128)S(1)} %fusion.30), channel_id=1, replica_groups=mesh['tier'=4,'tile'=8] {'tile'}, use_global_device_ids=true, to_apply=%region_7.8 | all-reduce | flops 16 | bytes 128 | tf_op jit(solution)/shard_map/psum | solution.py:88
  97.2 0.0 copy-start.4
  97.2 0.2 fusion.2
  97.4 0.1 slice.219
  97.5 6.6 %collective-permute-start.4 = (f32[1,24,1024]{2,1,0:T(8,128)S(1)}, f32[1,24,1024]{2,1,0:T(8,128)S(1)}, u32[]{:S(2)}, u32[]{:S(2)}) collective-permute-start(f32[1,24,1024]{2,1,0:T(8,128)S(1)} %slice.219), channel_id=1, source_target_pairs={{1,0},{2,1},{3,2},{4,3},{5,4},{6,5},{7,6},{9,8},{10,9},{11,10},{12... | collective-permute-start | bytes 294920 | tf_op jit(solution)/shard_map/ppermute | solution.py:20
  104.1 1.9 %collective-permute-start.5 = (f32[1,24,1024]{2,1,0:T(8,128)S(1)}, f32[1,24,1024]{2,1,0:T(8,128)S(1)}, u32[]{:S(2)}, u32[]{:S(2)}) collective-permute-start(f32[1,24,1024]{2,1,0:T(8,128)S(1)} %slice.222), channel_id=1, source_target_pairs={{0,1},{1,2},{2,3},{3,4},{4,5},{5,6},{6,7},{8,9},{9,10},{10,11},{11... | collective-permute-start | bytes 294920 | tf_op jit(solution)/shard_map/ppermute | solution.py:17
  106.0 0.1 broadcast_bitcast_fusion
  106.1 0.2 collective-permute-done.4
  106.3 5.2 %collective-permute-done.5 = f32[1,24,1024]{2,1,0:T(8,128)S(1)} collective-permute-done((f32[1,24,1024]{2,1,0:T(8,128)S(1)}, f32[1,24,1024]{2,1,0:T(8,128)S(1)}, u32[]{:S(2)}, u32[]{:S(2)}) %collective-permute-start.5) | collective-permute-done | bytes 98336 | tf_op jit(solution)/shard_map/ppermute | solution.py:17
  111.5 0.2 select_maximum_fusion.3
  111.8 1.4 fusion.7
  113.2 0.3 scatter-add.9
  113.5 0.9 copy.92
  114.4 2.9 %reshape.126 = f32[4,1,24576]{2,1,0:T(1,128)S(1)} reshape(f32[1024,4,24]{2,1,0:T(4,128)S(1)} %bitcast.117) | data formatting | bytes 786432
  117.3 9.8 %all_to_all.74 = f32[4,1,24576]{2,1,0:T(1,128)S(1)} all-to-all(f32[4,1,24576]{2,1,0:T(1,128)S(1)} %reshape.126), channel_id=1, replica_groups=mesh['tier'=4,'tile'=8] {'tier'}, dimensions={0} | all-to-all | bytes 786432 | tf_op jit(solution)/shard_map/all_to_all | solution.py:130
  127.1 1.7 %reduce.11 = f32[4,24576]{1,0:T(4,128)S(1)} reduce(f32[4,1,24576]{2,1,0:T(1,128)S(1)} %all_to_all.74, f32[]{:T(128)} %broadcast.157), dimensions={1}, to_apply=%all_to_all.60.reduce_sub_computation | reduce | bytes 786436 | tf_op jit(solution)/shard_map/all_to_all | solution.py:130
  128.8 2.8 %reshape.127 = f32[1024,4,24]{2,1,0:T(4,128)S(1)} reshape(f32[4,24576]{1,0:T(4,128)S(1)} %reduce.11) | data formatting | bytes 786432
  131.6 0.8 copy.93
  132.4 0.5 convolution_bitcast_fusion
  132.9 0.3 copy.94
  133.2 9.8 %all_to_all.75 = f32[4,96,256]{2,0,1:T(4,128)S(1)} all-to-all(f32[4,96,256]{2,0,1:T(4,128)S(1)} %copy.94), channel_id=1, replica_groups=mesh['tier'=4,'tile'=8] {'tier'}, dimensions={1} | all-to-all | bytes 786432 | tf_op jit(solution)/shard_map/all_to_all | solution.py:133
  143.0 0.3 copy.95
  143.3 0.9 all_to_all.67
  (19 shorter events, 0.1 us)
Async XLA Ops:
  0.6 68.0 %copy-start = (f32[96,96]{1,0:T(8,128)S(1)}, f32[96,96]{1,0:T(8,128)}, u32[]{:S(2)}) copy-start(f32[96,96]{1,0:T(8,128)} %param.17) | copy-start | bytes 110596
  1.6 45.3 %collective-permute-start.3 = (f32[1,24,1024]{2,1,0:T(8,128)S(1)}, f32[1,24,1024]{2,1,0:T(8,128)S(1)}, u32[]{:S(2)}, u32[]{:S(2)}) collective-permute-start(f32[1,24,1024]{2,1,0:T(8,128)S(1)} %get-tuple-element.44), channel_id=1, source_target_pairs={{0,1},{1,2},{2,3},{3,4},{4,5},{5,6},{6,7},{8,9},{9,10},{10,11},{11... | collective-permute-start | bytes 294920 | tf_op jit(solution)/shard_map/ppermute | solution.py:17
  5.0 41.9 %collective-permute-start.1 = (f32[1,24,1024]{2,1,0:T(8,128)S(1)}, f32[1,24,1024]{2,1,0:T(8,128)S(1)}, u32[]{:S(2)}, u32[]{:S(2)}) collective-permute-start(f32[1,24,1024]{2,1,0:T(8,128)S(1)} %get-tuple-element.45), channel_id=1, source_target_pairs={{1,0},{2,1},{3,2},{4,3},{5,4},{6,5},{7,6},{9,8},{10,9},{11,10},{12... | collective-permute-start | bytes 294920 | tf_op jit(solution)/shard_map/ppermute | solution.py:20
  16.9 12.2 %copy-start.3 = (f32[4,24,1024]{2,1,0:T(8,128)S(1)}, f32[4,24,1024]{2,1,0:T(8,128)}, u32[]{:S(2)}) copy-start(f32[4,24,1024]{2,1,0:T(8,128)} %param.11) | copy-start | bytes 1179652
  16.9 12.2 %copy-start.7 = (s32[1,8]{1,0:T(1,128)S(1)}, s32[1,8]{1,0:T(1,128)}, u32[]{:S(2)}) copy-start(s32[1,8]{1,0:T(1,128)} %param.14) | copy-start | bytes 100
  16.9 29.7 %copy-start.5 = (f32[4,16]{1,0:T(4,128)S(1)}, f32[4,16]{1,0:T(4,128)}, u32[]{:S(2)}) copy-start(f32[4,16]{1,0:T(4,128)} %param.15) | copy-start | bytes 772
  16.9 29.7 %copy-start.6 = (f32[4,16]{1,0:T(4,128)S(1)}, f32[4,16]{1,0:T(4,128)}, u32[]{:S(2)}) copy-start(f32[4,16]{1,0:T(4,128)} %param.16) | copy-start | bytes 772
  22.4 24.8 %collective-permute-start.2 = (f32[2,1,24,1024]{3,2,1,0:T(8,128)S(1)}, f32[2,1,24,1024]{3,2,1,0:T(8,128)S(1)}, u32[]{:S(2)}, u32[]{:S(2)}) collective-permute-start(f32[2,1,24,1024]{3,2,1,0:T(8,128)S(1)} %get-tuple-element.40), channel_id=1, source_target_pairs={{0,1},{1,2},{2,3},{3,4},{4,5},{5,6},{6,7},{8,9},{9,10},{10,11},{11... | collective-permute-start | bytes 589832 | tf_op jit(solution)/shard_map/ppermute | solution.py:17
  24.9 22.3 %collective-permute-start = (f32[2,1,24,1024]{3,2,1,0:T(8,128)S(1)}, f32[2,1,24,1024]{3,2,1,0:T(8,128)S(1)}, u32[]{:S(2)}, u32[]{:S(2)}) collective-permute-start(f32[2,1,24,1024]{3,2,1,0:T(8,128)S(1)} %get-tuple-element.41), channel_id=1, source_target_pairs={{1,0},{2,1},{3,2},{4,3},{5,4},{6,5},{7,6},{9,8},{10,9},{11,10},{12... | collective-permute-start | bytes 589832 | tf_op jit(solution)/shard_map/ppermute | solution.py:20
  47.6 1.3 copy-start.1
  79.5 32.3 %copy-start.2 = (f32[2,6,24,1026]{3,2,1,0:T(8,128)S(1)}, f32[2,6,24,1026]{3,2,1,0:T(8,128)}, u32[]{:S(2)}) copy-start(f32[2,6,24,1026]{3,2,1,0:T(8,128)} %copy-done.1) | copy-start | bytes 3545860
  97.2 16.0 %copy-start.4 = (f32[1,16]{1,0:T(1,128)}, f32[1,16]{1,0:T(1,128)S(1)}, u32[]{:S(2)}) copy-start(f32[1,16]{1,0:T(1,128)S(1)} %exponential_multiply_fusion) | copy-start | bytes 196
  97.5 8.8 %collective-permute-start.4 = (f32[1,24,1024]{2,1,0:T(8,128)S(1)}, f32[1,24,1024]{2,1,0:T(8,128)S(1)}, u32[]{:S(2)}, u32[]{:S(2)}) collective-permute-start(f32[1,24,1024]{2,1,0:T(8,128)S(1)} %slice.219), channel_id=1, source_target_pairs={{1,0},{2,1},{3,2},{4,3},{5,4},{6,5},{7,6},{9,8},{10,9},{11,10},{12... | collective-permute-start | bytes 294920 | tf_op jit(solution)/shard_map/ppermute | solution.py:20
  104.1 7.4 %collective-permute-start.5 = (f32[1,24,1024]{2,1,0:T(8,128)S(1)}, f32[1,24,1024]{2,1,0:T(8,128)S(1)}, u32[]{:S(2)}, u32[]{:S(2)}) collective-permute-start(f32[1,24,1024]{2,1,0:T(8,128)S(1)} %slice.222), channel_id=1, source_target_pairs={{0,1},{1,2},{2,3},{3,4},{4,5},{5,6},{6,7},{8,9},{9,10},{10,11},{11... | collective-permute-start | bytes 294920 | tf_op jit(solution)/shard_map/ppermute | solution.py:17
where the time goes:
time: 145 us; the launch traced here: 144 us
  blocking collectives  73.7 us (51%)
  starting transfers between devices  22 us (15%)
  local copies, waits for them, and re-layouts  21 us (14%)
  other arithmetic  19.3 us (13%)
  waiting for transfers between devices  5.42 us (4%)
  matrix products  1.71 us (1%)
    psum x2, blocking collectives, leak_tiers(): block_sum, block_count = lax.psum((partial_value[0], counts), 'tile')  34.2 us
    all_to_all x2, blocking collectives, shards(): lax.all_to_all(moved_field, 'tier', split_axis=2, concat_axis=1, tiled=True)  19.8 us
    all_to_all x2, blocking collectives, shards(): lax.all_to_all(applied, 'tier', split_axis=1, concat_axis=2, tiled=True)  19.7 us
    ppermute x3, starting transfers between devices, extended(): lax.ppermute(lax.slice_in_dim(block, 0, width, axis=dim), axis, backward)  14.1 us
    unnamed x20, local copies, waits for them, and re-layouts  11.4 us
    ppermute x3, starting transfers between devices, extended(): lax.ppermute(lax.slice_in_dim(block, block.shape[dim] - width, None, axis...  7.88 us
    select_n x1, other arithmetic, lookup_codes(): jnp.where(is_material, material_transport_rates[1, material], stacking_co...  6.55 us
    select_n x1, other arithmetic, lookup_codes(): jnp.where(is_material, material_transport_rates[0, material], sideways_co...  5.36 us
  transfers between devices with their start and end apart: 6, of which 2 were waited for; matrix products, arithmetic and copies ran while one was open for 10% of the time, Pallas kernels for 0%

commit v1 on v0

--- a/solution.py
+++ b/solution.py
@@ -7,6 +7,17 @@
 STEPS = 2
 LATERAL_RATE = 0.12
 SOURCE_GAIN = 0.02
+
+
+def split_up(value, dim, length):
+    before, after = (value.shape[:dim], value.shape[dim + 1 :])
+    return jnp.moveaxis(value.reshape(*before, length, -1, *after), dim, 0)
+
+
+def laid_out(tiles, dim):
+    tiles = jnp.moveaxis(tiles, 0, dim)
+    dims = tiles.shape
+    return tiles.reshape(*dims[:dim], dims[dim] * dims[dim + 1], *dims[dim + 2 :])
 
 
 def extended(block, sides, width):
@@ -130,9 +141,14 @@
             lax.all_to_all(moved_field, "tier", split_axis=2, concat_axis=1, tiled=True),
             precision=lax.Precision.HIGHEST,
         )
-        present_warming_state = lax.all_to_all(
-            applied, "tier", split_axis=1, concat_axis=2, tiled=True
-        )
+        size, mine = (lax.axis_size("tier"), lax.axis_index("tier"))
+        blocks = split_up(applied, 1, size)
+        finished = [blocks[mine]]
+        for lap in range(1, size):
+            sent = blocks[mine ^ lap]
+            finished.append(lax.ppermute(sent, "tier", [(i_2, i_2 ^ lap) for i_2 in range(size)]))
+        blocks = jnp.stack(finished)[mine ^ jnp.arange(size)]
+        present_warming_state = laid_out(blocks, 2)
     return (present_warming_state, power_row)
 
 

time: 145 us -> 135 us (0.931)
  the two profiles are of different devices: /device:TPU:8 before, /device:TPU:0 now
where the time goes in v1:
time: 135 us; the launch traced here: 134 us
  blocking collectives  47.2 us (35%)
  starting transfers between devices  26.8 us (20%)
  local copies, waits for them, and re-layouts  20.6 us (15%)
  other arithmetic  19.1 us (14%)
  waiting for transfers between devices  17.4 us (13%)
  matrix products  1.71 us (1%)
    psum x2, blocking collectives, leak_tiers(): block_sum, block_count = lax.psum((partial_value[0], counts), 'tile')  37.4 us
    ppermute x3, starting transfers between devices, extended(): lax.ppermute(lax.slice_in_dim(block, block.shape[dim] - width, None, axis...  15.5 us
    unnamed x21, local copies, waits for them, and re-layouts  12.1 us
    ppermute x6, waiting for transfers between devices, shards(): lax.ppermute(sent, 'tier', [(i_2, i_2 ^ lap) for i_2 in range(size)])  9.99 us
    all_to_all x1, blocking collectives, shards(): lax.all_to_all(moved_field, 'tier', split_axis=2, concat_axis=1, tiled=True)  9.84 us
    all_to_all x1, waiting for transfers between devices, shards(): lax.all_to_all(moved_field, 'tier', split_axis=2, concat_axis=1, tiled=True)  7.38 us
    select_n x1, other arithmetic, lookup_codes(): jnp.where(is_material, material_transport_rates[1, material], stacking_co...  6.46 us
    select_n x1, other arithmetic, lookup_codes(): jnp.where(is_material, material_transport_rates[0, material], sideways_co...  5.32 us
  transfers between devices with their start and end apart: 13, of which 5 were waited for; matrix products, arithmetic and copies ran while one was open for 1% of the time, Pallas kernels for 0%

profile of v1, /device:TPU:0, one launch (start us, length us, event | category | flops | bytes accessed | tf_op | source)
XLA Modules:
  0.0 133.9 jit_solution(5757139597803868348)
XLA Ops:
  0.6 0.0 copy-start
  0.6 2.0 %fusion.44 = (f32[1,1]{1,0:T(1,128)}, f32[1,1]{1,0:T(1,128)}, f32[1,1]{1,0:T(1,128)}, f32[1,1]{1,0:T(1,128)}, f32[1,1]{1,0:T(1,128)}, /*index=5*/f32[1,1]{1,0:T(...) fusion(f32[2,8]{1,0:T(2,128)} %param.13), kind=kLoop, calls=%fused_computation.120 | loop fusion | bytes 128 | tf_op jit(solution)/shard_map/slice | solution.py:71
  2.6 6.5 %select_select_fusion = (f32[4,24,1024]{2,1,0:T(8,128)S(1)}, pred[4,24,1024]{2,1,0:T(8,128)(4,1)S(1)}, pred[4,24,1024]{2,1,0:T(8,128)(4,1)S(1)}, pred[4,24,1024]...) fusion(f32[]{:T(128)} %bitcast.16, f32[]{:T(128)} %bitcast.15, ...), kind=kLoop, calls=%fused_computation.63 | loop fusion | flops 1671168 | bytes 1572896 | tf_op jit(solution)/shard_map/jit(_where)/select_n | solution.py:73
  9.1 0.0 copy-start.3
  9.1 0.0 copy-start.7
  9.1 0.0 copy-start.5
  9.1 0.0 copy-start.6
  9.1 5.3 %select_select_fusion.1 = f32[4,24,1024]{2,1,0:T(8,128)S(1)} fusion(pred[4,24,1024]{2,1,0:T(8,128)(4,1)S(1)} %get-tuple-element.39, pred[4,24,1024]{2,1,0:T(8,128)(4,1)S(1)} %get-tuple-element.38, pred[4,24,1024]{2,1,0:T(8,128)(4,1)S(1)} %get-tuple-element.37, pred[4,24,1024]{2,1,0:T(8,128)(4,1)S(1)} %get-tuple-element.36, ...), kind=kLoop, calls=%fused_computation.64 | loop fusion | flops 786432 | bytes 1179680 | tf_op jit(solution)/shard_map/jit(_where)/select_n | solution.py:70
  14.5 1.3 collective-permute-start
  15.8 5.5 %collective-permute-start.2 = (f32[2,1,24,1024]{3,2,1,0:T(8,128)S(1)}, f32[2,1,24,1024]{3,2,1,0:T(8,128)S(1)}, u32[]{:S(2)}, u32[]{:S(2)}) collective-permute-start(f32[2,1,24,1024]{3,2,1,0:T(8,128)S(1)} %get-tuple-element.40), channel_id=1, source_target_pairs={{0,1},{1,2},{2,3},{3,4},{4,5},{5,6},{6,7},{8,9},{9,10},{10,11},{11... | collective-permute-start | bytes 589832 | tf_op jit(solution)/shard_map/ppermute | solution.py:28
  21.4 1.3 collective-permute-start.1
  22.7 5.4 %collective-permute-start.3 = (f32[1,24,1024]{2,1,0:T(8,128)S(1)}, f32[1,24,1024]{2,1,0:T(8,128)S(1)}, u32[]{:S(2)}, u32[]{:S(2)}) collective-permute-start(f32[1,24,1024]{2,1,0:T(8,128)S(1)} %get-tuple-element.52), channel_id=1, source_target_pairs={{0,1},{1,2},{2,3},{3,4},{4,5},{5,6},{6,7},{8,9},{9,10},{10,11},{11... | collective-permute-start | bytes 294920 | tf_op jit(solution)/shard_map/ppermute | solution.py:28
  28.1 0.1 bitcast_reduce_fusion.1
  28.3 0.1 convert_reduce_fusion
  28.3 0.2 fusion.33
  28.5 20.2 %all-reduce.3 = (f32[1,16]{1,0:T(1,128)S(1)}, f32[1,16]{1,0:T(1,128)S(1)}) all-reduce(f32[1,16]{1,0:T(1,128)S(1)} %multiply_bitcast_fusion.2, f32[1,16]{1,0:T(1,128)S(1)} %fusion.33), channel_id=1, replica_groups=mesh['tier'=4,'tile'=8] {'tile'}, use_global_device_ids=true, to_apply=%region_4.5 | all-reduce | flops 32 | bytes 256 | tf_op jit(solution)/shard_map/psum | solution.py:99
  48.8 0.2 fusion.1
  49.0 0.1 broadcast_bitcast_fusion.1
  49.0 0.3 select_maximum_fusion.5
  49.3 0.4 select_maximum_fusion
  49.7 1.2 fusion.18
  51.0 0.1 scatter-add.6
  51.2 0.9 copy.27
  52.0 3.6 %reshape.186 = f32[4,1,24576]{2,1,0:T(1,128)} reshape(f32[1024,4,24]{2,1,0:T(4,128)S(1)} %bitcast.146) | data formatting | bytes 786432
  55.7 3.5 %all-to-all-start = ((f32[4,1,24576]{2,1,0:T(1,128)}), f32[4,1,24576]{2,1,0:T(1,128)S(1)}, u32[]{:S(2)}, u32[]{:S(2)}) async-start(f32[4,1,24576]{2,1,0:T(1,128)} %reshape.186), calls=%async_computation | async-start | bytes 786432 | tf_op jit(solution)/shard_map/all_to_all | solution.py:141
  59.2 7.4 %all-to-all-done = f32[4,1,24576]{2,1,0:T(1,128)S(1)} async-done(((f32[4,1,24576]{2,1,0:T(1,128)}), f32[4,1,24576]{2,1,0:T(1,128)S(1)}, u32[]{:S(2)}, u32[]{:S(2)}) %all-to-all-start) | async-done | bytes 393248 | tf_op jit(solution)/shard_map/all_to_all | solution.py:141
  66.5 0.5 broadcast.194
  67.0 1.7 %reduce.10 = f32[4,24576]{1,0:T(4,128)S(1)} reduce(f32[4,1,24576]{2,1,0:T(1,128)S(1)} %all-to-all-done, f32[]{:T(128)} %broadcast.194), dimensions={1}, to_apply=%all_to_all.26.reduce_sub_computation | reduce | bytes 786436 | tf_op jit(solution)/shard_map/all_to_all | solution.py:141
  68.7 2.8 %reshape.187 = f32[1024,4,24]{2,1,0:T(4,128)S(1)} reshape(f32[4,24576]{1,0:T(4,128)S(1)} %reduce.10) | data formatting | bytes 786432
  71.5 0.8 copy.28
  72.2 0.5 fusion.30
  72.8 0.1 collective-permute-start.4
  72.9 0.4 collective-permute-start.5
  73.3 1.4 %collective-permute-start.6 = (f32[4,24,256]{2,1,0:T(8,128)S(1)}, f32[4,24,256]{2,1,0:T(8,128)S(1)}, u32[]{:S(2)}, u32[]{:S(2)}) collective-permute-start(f32[4,24,256]{2,1,0:T(8,128)S(1)} %get-tuple-element.49), channel_id=1, source_target_pairs={{0,24},{8,16},{16,8},{24,0},{1,25},{9,17},{17,9},{25,1},{2,26},{10... | collective-permute-start | bytes 294920 | tf_op jit(solution)/shard_map/ppermute | solution.py:149
  74.7 0.0 collective-permute-done.4
  74.7 3.8 %collective-permute-done.5 = f32[4,24,256]{2,1,0:T(8,128)S(1)} collective-permute-done((f32[4,24,256]{2,1,0:T(8,128)S(1)}, f32[4,24,256]{2,1,0:T(8,128)S(1)}, u32[]{:S(2)}, u32[]{:S(2)}) %collective-permute-start.5) | collective-permute-done | bytes 98336 | tf_op jit(solution)/shard_map/ppermute | solution.py:149
  78.5 1.2 collective-permute-done.6
  79.8 0.6 gather_fusion
  80.4 1.4 %collective-permute-start.7 = (f32[1,24,1024]{2,1,0:T(8,128)S(1)}, f32[1,24,1024]{2,1,0:T(8,128)S(1)}, u32[]{:S(2)}, u32[]{:S(2)}) collective-permute-start(f32[1,24,1024]{2,1,0:T(8,128)S(1)} %bitcast.167), channel_id=1, source_target_pairs={{1,0},{2,1},{3,2},{4,3},{5,4},{6,5},{7,6},{9,8},{10,9},{11,10},{12... | collective-permute-start | bytes 294920 | tf_op jit(solution)/shard_map/ppermute | solution.py:31
  81.9 0.1 bitcast_reduce_fusion
  82.0 0.2 fusion.32
  82.2 4.5 %collective-permute-start.8 = (f32[1,24,1024]{2,1,0:T(8,128)S(1)}, f32[1,24,1024]{2,1,0:T(8,128)S(1)}, u32[]{:S(2)}, u32[]{:S(2)}) collective-permute-start(f32[1,24,1024]{2,1,0:T(8,128)S(1)} %bitcast.168), channel_id=1, source_target_pairs={{0,1},{1,2},{2,3},{3,4},{4,5},{5,6},{6,7},{8,9},{9,10},{10,11},{11... | collective-permute-start | bytes 294920 | tf_op jit(solution)/shard_map/ppermute | solution.py:28
  86.8 17.1 %psum.26 = f32[1,16]{1,0:T(1,128)S(1)} all-reduce(f32[1,16]{1,0:T(1,128)S(1)} %fusion.32), channel_id=1, replica_groups=mesh['tier'=4,'tile'=8] {'tile'}, use_global_device_ids=true, to_apply=%region_7.8 | all-reduce | flops 16 | bytes 128 | tf_op jit(solution)/shard_map/psum | solution.py:99
  103.9 0.0 copy-start.4
  103.9 0.2 fusion.2
  104.1 0.1 broadcast_bitcast_fusion
  104.2 0.0 collective-permute-done.7
  104.2 0.2 select_maximum_fusion.3
  104.4 1.4 %fusion.7 = f32[4,24,1024]{2,1,0:T(8,128)S(1)} fusion(f32[4,24,1024]{2,1,0:T(8,128)S(1)} %bitcast.152, f32[6,24,1026]{2,1,0:T(8,128)S(1)} %select_maximum_fusion.3, f32[4,24,1024]{2,1,0:T(8,128)} %get-tuple-element.30, f32[1,24,1024]{2,1,0:T(8,128)S(1)} %collective-permute-done.8, f32[4,24,1024]{2,1,0:T(8,128)S(1)} %get-tuple-element.29, ...), kind=kLoop, calls=%fused_computation.23 | loop fusion | flops 2162688 | bytes 3735552 | tf_op jit(solution)/shard_map/add | solution.py:56
  105.9 0.3 scatter-add.9
  106.2 0.9 copy.32
  107.1 2.9 %reshape.188 = f32[4,1,24576]{2,1,0:T(1,128)S(1)} reshape(f32[1024,4,24]{2,1,0:T(4,128)S(1)} %bitcast.148) | data formatting | bytes 786432
  110.0 9.8 %all_to_all.36 = f32[4,1,24576]{2,1,0:T(1,128)S(1)} all-to-all(f32[4,1,24576]{2,1,0:T(1,128)S(1)} %reshape.188), channel_id=1, replica_groups=mesh['tier'=4,'tile'=8] {'tier'}, dimensions={0} | all-to-all | bytes 786432 | tf_op jit(solution)/shard_map/all_to_all | solution.py:141
  119.8 1.7 %reduce.11 = f32[4,24576]{1,0:T(4,128)S(1)} reduce(f32[4,1,24576]{2,1,0:T(1,128)S(1)} %all_to_all.36, f32[]{:T(128)} %broadcast.194), dimensions={1}, to_apply=%all_to_all.30.reduce_sub_computation | reduce | bytes 786436 | tf_op jit(solution)/shard_map/all_to_all | solution.py:141
  121.4 2.8 %reshape.189 = f32[1024,4,24]{2,1,0:T(4,128)S(1)} reshape(f32[4,24576]{1,0:T(4,128)S(1)} %reduce.11) | data formatting | bytes 786432
  124.2 0.8 copy.33
  125.0 0.5 fusion.28
  125.6 0.1 collective-permute-start.9
  125.6 0.4 collective-permute-start.10
  126.1 1.4 %collective-permute-start.11 = (f32[4,24,256]{2,1,0:T(8,128)S(1)}, f32[4,24,256]{2,1,0:T(8,128)S(1)}, u32[]{:S(2)}, u32[]{:S(2)}) collective-permute-start(f32[4,24,256]{2,1,0:T(8,128)S(1)} %get-tuple-element.43), channel_id=1, source_target_pairs={{0,24},{8,16},{16,8},{24,0},{1,25},{9,17},{17,9},{25,1},{2,26},{10... | collective-permute-start | bytes 294920 | tf_op jit(solution)/shard_map/ppermute | solution.py:149
  127.5 3.8 %collective-permute-done.10 = f32[4,24,256]{2,1,0:T(8,128)S(1)} collective-permute-done((f32[4,24,256]{2,1,0:T(8,128)S(1)}, f32[4,24,256]{2,1,0:T(8,128)S(1)}, u32[]{:S(2)}, u32[]{:S(2)}) %collective-permute-start.10) | collective-permute-done | bytes 98336 | tf_op jit(solution)/shard_map/ppermute | solution.py:149
  131.3 1.2 collective-permute-done.11
  132.5 0.6 gather_fusion.1
  133.1 0.8 copy.38
  (34 shorter events, 0.4 us)
Async XLA Ops:
  0.6 71.6 %copy-start = (f32[96,96]{1,0:T(8,128)S(1)}, f32[96,96]{1,0:T(8,128)}, u32[]{:S(2)}) copy-start(f32[96,96]{1,0:T(8,128)} %param.17) | copy-start | bytes 110596
  9.1 12.2 %copy-start.3 = (f32[4,24,1024]{2,1,0:T(8,128)S(1)}, f32[4,24,1024]{2,1,0:T(8,128)}, u32[]{:S(2)}) copy-start(f32[4,24,1024]{2,1,0:T(8,128)} %param.11) | copy-start | bytes 1179652
  9.1 19.1 %copy-start.7 = (s32[1,8]{1,0:T(1,128)S(1)}, s32[1,8]{1,0:T(1,128)}, u32[]{:S(2)}) copy-start(s32[1,8]{1,0:T(1,128)} %param.14) | copy-start | bytes 100
  9.1 39.7 %copy-start.5 = (f32[4,16]{1,0:T(4,128)S(1)}, f32[4,16]{1,0:T(4,128)}, u32[]{:S(2)}) copy-start(f32[4,16]{1,0:T(4,128)} %param.15) | copy-start | bytes 772
  9.1 39.7 %copy-start.6 = (f32[4,16]{1,0:T(4,128)S(1)}, f32[4,16]{1,0:T(4,128)}, u32[]{:S(2)}) copy-start(f32[4,16]{1,0:T(4,128)} %param.16) | copy-start | bytes 772
  14.5 34.8 %collective-permute-start = (f32[2,1,24,1024]{3,2,1,0:T(8,128)S(1)}, f32[2,1,24,1024]{3,2,1,0:T(8,128)S(1)}, u32[]{:S(2)}, u32[]{:S(2)}) collective-permute-start(f32[2,1,24,1024]{3,2,1,0:T(8,128)S(1)} %get-tuple-element.41), channel_id=1, source_target_pairs={{1,0},{2,1},{3,2},{4,3},{5,4},{6,5},{7,6},{9,8},{10,9},{11,10},{12... | collective-permute-start | bytes 589832 | tf_op jit(solution)/shard_map/ppermute | solution.py:31
  15.8 33.5 %collective-permute-start.2 = (f32[2,1,24,1024]{3,2,1,0:T(8,128)S(1)}, f32[2,1,24,1024]{3,2,1,0:T(8,128)S(1)}, u32[]{:S(2)}, u32[]{:S(2)}) collective-permute-start(f32[2,1,24,1024]{3,2,1,0:T(8,128)S(1)} %get-tuple-element.40), channel_id=1, source_target_pairs={{0,1},{1,2},{2,3},{3,4},{4,5},{5,6},{6,7},{8,9},{9,10},{10,11},{11... | collective-permute-start | bytes 589832 | tf_op jit(solution)/shard_map/ppermute | solution.py:28
  21.4 27.7 %collective-permute-start.1 = (f32[1,24,1024]{2,1,0:T(8,128)S(1)}, f32[1,24,1024]{2,1,0:T(8,128)S(1)}, u32[]{:S(2)}, u32[]{:S(2)}) collective-permute-start(f32[1,24,1024]{2,1,0:T(8,128)S(1)} %get-tuple-element.53), channel_id=1, source_target_pairs={{1,0},{2,1},{3,2},{4,3},{5,4},{6,5},{7,6},{9,8},{10,9},{11,10},{12... | collective-permute-start | bytes 294920 | tf_op jit(solution)/shard_map/ppermute | solution.py:31
  22.7 26.4 %collective-permute-start.3 = (f32[1,24,1024]{2,1,0:T(8,128)S(1)}, f32[1,24,1024]{2,1,0:T(8,128)S(1)}, u32[]{:S(2)}, u32[]{:S(2)}) collective-permute-start(f32[1,24,1024]{2,1,0:T(8,128)S(1)} %get-tuple-element.52), channel_id=1, source_target_pairs={{0,1},{1,2},{2,3},{3,4},{4,5},{5,6},{6,7},{8,9},{9,10},{10,11},{11... | collective-permute-start | bytes 294920 | tf_op jit(solution)/shard_map/ppermute | solution.py:28
  49.7 1.3 copy-start.1
  55.7 10.9 %all-to-all-start = ((f32[4,1,24576]{2,1,0:T(1,128)}), f32[4,1,24576]{2,1,0:T(1,128)S(1)}, u32[]{:S(2)}, u32[]{:S(2)}) async-start(f32[4,1,24576]{2,1,0:T(1,128)} %reshape.186), calls=%async_computation | async-start | bytes 786432 | tf_op jit(solution)/shard_map/all_to_all | solution.py:141
  72.8 1.9 %collective-permute-start.4 = (f32[4,24,256]{2,1,0:T(8,128)S(1)}, f32[4,24,256]{2,1,0:T(8,128)S(1)}, u32[]{:S(2)}, u32[]{:S(2)}) collective-permute-start(f32[4,24,256]{2,1,0:T(8,128)S(1)} %get-tuple-element.51), channel_id=1, source_target_pairs={{0,8},{8,0},{16,24},{24,16},{1,9},{9,1},{17,25},{25,17},{2,10},{10... | collective-permute-start | bytes 294920 | tf_op jit(solution)/shard_map/ppermute | solution.py:149
  72.9 5.7 %collective-permute-start.5 = (f32[4,24,256]{2,1,0:T(8,128)S(1)}, f32[4,24,256]{2,1,0:T(8,128)S(1)}, u32[]{:S(2)}, u32[]{:S(2)}) collective-permute-start(f32[4,24,256]{2,1,0:T(8,128)S(1)} %get-tuple-element.50), channel_id=1, source_target_pairs={{0,16},{8,24},{16,0},{24,8},{1,17},{9,25},{17,1},{25,9},{2,18},{10... | collective-permute-start | bytes 294920 | tf_op jit(solution)/shard_map/ppermute | solution.py:149
  73.3 6.4 %collective-permute-start.6 = (f32[4,24,256]{2,1,0:T(8,128)S(1)}, f32[4,24,256]{2,1,0:T(8,128)S(1)}, u32[]{:S(2)}, u32[]{:S(2)}) collective-permute-start(f32[4,24,256]{2,1,0:T(8,128)S(1)} %get-tuple-element.49), channel_id=1, source_target_pairs={{0,24},{8,16},{16,8},{24,0},{1,25},{9,17},{17,9},{25,1},{2,26},{10... | collective-permute-start | bytes 294920 | tf_op jit(solution)/shard_map/ppermute | solution.py:149
  80.4 24.1 %copy-start.2 = (f32[2,6,24,1026]{3,2,1,0:T(8,128)S(1)}, f32[2,6,24,1026]{3,2,1,0:T(8,128)}, u32[]{:S(2)}) copy-start(f32[2,6,24,1026]{3,2,1,0:T(8,128)} %copy-done.1) | copy-start | bytes 3545860
  80.4 23.8 %collective-permute-start.7 = (f32[1,24,1024]{2,1,0:T(8,128)S(1)}, f32[1,24,1024]{2,1,0:T(8,128)S(1)}, u32[]{:S(2)}, u32[]{:S(2)}) collective-permute-start(f32[1,24,1024]{2,1,0:T(8,128)S(1)} %bitcast.167), channel_id=1, source_target_pairs={{1,0},{2,1},{3,2},{4,3},{5,4},{6,5},{7,6},{9,8},{10,9},{11,10},{12... | collective-permute-start | bytes 294920 | tf_op jit(solution)/shard_map/ppermute | solution.py:31
  82.2 22.0 %collective-permute-start.8 = (f32[1,24,1024]{2,1,0:T(8,128)S(1)}, f32[1,24,1024]{2,1,0:T(8,128)S(1)}, u32[]{:S(2)}, u32[]{:S(2)}) collective-permute-start(f32[1,24,1024]{2,1,0:T(8,128)S(1)} %bitcast.168), channel_id=1, source_target_pairs={{0,1},{1,2},{2,3},{3,4},{4,5},{5,6},{6,7},{8,9},{9,10},{10,11},{11... | collective-permute-start | bytes 294920 | tf_op jit(solution)/shard_map/ppermute | solution.py:28
  103.9 1.9 %copy-start.4 = (f32[1,16]{1,0:T(1,128)}, f32[1,16]{1,0:T(1,128)S(1)}, u32[]{:S(2)}) copy-start(f32[1,16]{1,0:T(1,128)S(1)} %exponential_multiply_fusion) | copy-start | bytes 196
  125.6 1.9 %collective-permute-start.9 = (f32[4,24,256]{2,1,0:T(8,128)S(1)}, f32[4,24,256]{2,1,0:T(8,128)S(1)}, u32[]{:S(2)}, u32[]{:S(2)}) collective-permute-start(f32[4,24,256]{2,1,0:T(8,128)S(1)} %get-tuple-element.45), channel_id=1, source_target_pairs={{0,8},{8,0},{16,24},{24,16},{1,9},{9,1},{17,25},{25,17},{2,10},{10... | collective-permute-start | bytes 294920 | tf_op jit(solution)/shard_map/ppermute | solution.py:149
  125.6 5.7 %collective-permute-start.10 = (f32[4,24,256]{2,1,0:T(8,128)S(1)}, f32[4,24,256]{2,1,0:T(8,128)S(1)}, u32[]{:S(2)}, u32[]{:S(2)}) collective-permute-start(f32[4,24,256]{2,1,0:T(8,128)S(1)} %get-tuple-element.44), channel_id=1, source_target_pairs={{0,16},{8,24},{16,0},{24,8},{1,17},{9,25},{17,1},{25,9},{2,18},{10... | collective-permute-start | bytes 294920 | tf_op jit(solution)/shard_map/ppermute | solution.py:149
  126.1 6.4 %collective-permute-start.11 = (f32[4,24,256]{2,1,0:T(8,128)S(1)}, f32[4,24,256]{2,1,0:T(8,128)S(1)}, u32[]{:S(2)}, u32[]{:S(2)}) collective-permute-start(f32[4,24,256]{2,1,0:T(8,128)S(1)} %get-tuple-element.43), channel_id=1, source_target_pairs={{0,24},{8,16},{16,8},{24,0},{1,25},{9,17},{17,9},{25,1},{2,26},{10... | collective-permute-start | bytes 294920 | tf_op jit(solution)/shard_map/ppermute | solution.py:149
